TPU v7x, 32 devices: a whole 2x2x4 slice. The times are simulated.
32 devices in a mesh: tile: 16 (over z, x, core), pgrp: 2 (over y).
Axes of the slice: x: 2, y: 2, z: 4, core: 2. Of those that a mesh axis runs over, the one named last changes fastest.
Arguments:
- concentrations: float32 [130, 16, 256], P(None, 'tile'), may hold values from 0.1 to 2
- tangents: float32 [64, 130, 16, 256], P('pgrp', None, 'tile'), may hold values from -6 to 6
- rates: float32 [218, 16, 256], P(None, 'tile'), may hold values from 0.01 to 1
- substeps: int32 [16, 256], P('tile'), may hold values from 1 to 4, as said below
- courant: float32 [2, 16, 256], P(None, 'tile'), may hold values from -0.9 to 0.9
- reactants: int32 [218, 2], replicated, may hold values from 0 to 129
- products: int32 [218, 2], replicated, may hold values from 0 to 129
- yields: float32 [218, 2], replicated, may hold values from 0.2 to 0.5
- reaction_index: int32 [64], P('pgrp'), may hold values from 0 to 217
Outputs:
- concentrations_out: float32 [130, 16, 256], P(None, 'tile')
- tangents_out: float32 [64, 130, 16, 256], P('pgrp', None, 'tile')
Inputs may be any that keep to these rules, and one draw needn't show every extreme that they name: `substeps`: each column needs at least one substep; some column has 4.
All inputs are finite; a program needn't handle non-finite values.
Results may differ from a plain program's by a relative error of at most 0.0003.
Values sent between devices are 32-bit elements; how exact they have to be, the bound alone decides.
No kernel may reach another device: no remote copies, remote signals or barrier semaphores. Data moves between devices by JAX's collectives and lax.ppermute only.
A program may use at most 256 MiB of HBM per device.

v0:
```python
import functools
import math

import jax
import jax.numpy as jnp
import numpy as np
from jax import lax
from jax.experimental import pallas as pl
from jax.experimental.pallas import tpu as pltpu
from jax.sharding import PartitionSpec as P

CX = 16
CY = 16
NMAX = 4
LANES = 128
UNROLL = 32
BUFFERS = 2
SPLIT = 2
VMEM_LIMIT = 36 * 2**20
F32 = jnp.float32
BF16 = jnp.bfloat16


def orders():
    last, end = CX - 2, CY - 2
    west = [(i, j) for i in range(2) for j in range(CY)]
    east = [(i, j) for i in range(last, CX) for j in range(CY)]
    south = [(i, j) for j in range(2) for i in range(CX)]
    north = [(i, j) for j in range(end, CY) for i in range(CX)]
    strips = west + east + south + north
    edge = list(dict.fromkeys(strips))
    inner = [(i, j) for i in range(CX) for j in range(CY) if (i, j) not in set(edge)]
    return edge + inner, strips


def one_hot(source, wanted):
    place = {cell: k for k, cell in enumerate(source)}
    table = np.zeros((len(source), len(wanted)), np.float32)
    for lane, cell in enumerate(wanted):
        if cell is not None:
            table[place[cell], lane] = 1.0
    return table


def static_tables():
    order, strips = orders()
    cells = [(i, j) for i in range(CX) for j in range(CY)]
    west = [(i - CX, j) for i, j in strips[32:64]]
    east = [(i + CX, j) for i, j in strips[0:32]]
    south = [(i, j - CY) for i, j in strips[96:128]]
    north = [(i, j + CY) for i, j in strips[64:96]]
    blocks = [order[32 * k : 32 * k + 32] for k in range(4)] + [west, east]
    side_in = [(i, j, q) for block in blocks for q in range(4) for i, j in block]
    own_sides = (strips[64:96], strips[96:128])
    side_out = [(i, j, q) for block in own_sides for q in range(4) for i, j in block]
    entries = order + west + east + south + north
    return {
        "permute": one_hot(cells, order),
        "side_pick": one_hot(cells, [(i, j) for i, j, _ in side_out]),
        "side_in": np.array(side_in, np.int32),
        "side_out": np.array(side_out, np.int32).T,
        "entries": np.array(entries, np.int32),
        "cells": np.array(cells, np.int32),
        "cells_rows": np.array(cells, np.int32).T,
    }


def dot(left, right):
    return jnp.dot(left, right, preferred_element_type=F32)


def parts_of(value, count):
    parts = []
    for k in range(count):
        part = value.astype(BF16)
        parts.append(part)
        if k + 1 < count:
            value = value - part.astype(F32)
    return parts


def select_left(exact, value, count):
    return sum(dot(exact, part) for part in parts_of(value, count))


def select_right(value, exact, count):
    return sum(dot(part, exact) for part in parts_of(value, count))


def product(left_parts, value):
    high, low = parts_of(value, 2)
    return dot(left_parts[0], high) + (dot(left_parts[0], low) + dot(left_parts[1], high))


def product_right(value, right_parts):
    high, low = parts_of(value, 2)
    return dot(high, right_parts[0]) + (dot(low, right_parts[0]) + dot(high, right_parts[1]))


def lane_of(rows):
    return lax.broadcasted_iota(jnp.int32, (rows, LANES), 1)


def swap_blocks(arrays):
    lane = lane_of(arrays[0].shape[0])
    low = lane < 64
    even = (lane // 32) % 2 == 0
    a, b, c, d = arrays
    a, c = (
        jnp.where(low, a, pltpu.roll(c, 64, 1)),
        jnp.where(low, pltpu.roll(a, 64, 1), c),
    )
    b, d = (
        jnp.where(low, b, pltpu.roll(d, 64, 1)),
        jnp.where(low, pltpu.roll(b, 64, 1), d),
    )
    a, b = (
        jnp.where(even, a, pltpu.roll(b, 32, 1)),
        jnp.where(even, pltpu.roll(a, 96, 1), b),
    )
    c, d = (
        jnp.where(even, c, pltpu.roll(d, 32, 1)),
        jnp.where(even, pltpu.roll(c, 96, 1), d),
    )
    return [a, b, c, d]


def tangent_copies(source, target, sems):
    return [
        pltpu.make_async_copy(source.at[p], target.at[:, p // 8, :, p % 8, :], sems.at[p // 8])
        for p in range(source.shape[0])
    ]


def up_to(value, step):
    return -(-value // step) * step


def rows_of(reactions, species):
    padded = up_to(species, 8)
    starts = [0, reactions, 2 * reactions]
    starts += [3 * reactions + k * padded for k in range(3)]
    return starts, 3 * reactions + 3 * padded


def tangent_chemistry(
    ilist, ylist, chosen, held, real, group, origin, t, x, used, made, start, stop
):
    species = t.shape[0] // group - 1
    reactions = up_to(real, 8)
    listed = ilist.shape[0] // 4
    at_a, at_b, at_flux, at_fd, at_fda, at_again = [at // 8 for at in rows_of(reactions, species)[0]]
    sublane = lax.broadcasted_iota(jnp.int32, (8, LANES), 0)

    def rows(place):
        return pl.ds(pl.multiple_of(place, group), group)

    def apply(source, n):
        def some(step, count):
            for k0 in range(0, count, BUFFERS):
                batch = range(k0, min(k0 + BUFFERS, count))
                mixes, places, olds = [], [], []
                for k in batch:
                    r = step * UNROLL + k
                    tile, k8 = step * (UNROLL // 8) + k // 8, k % 8
                    place = [rows(ilist[row * listed + r]) for row in range(4)]
                    mixes.append(
                        held[n, at_a + tile, k8 : k8 + 1, :] * source[place[0], :]
                        + held[n, at_b + tile, k8 : k8 + 1, :] * source[place[1], :]
                    )
                    places.append(place)
                for k, (i1, i2, q1, q2) in enumerate(places):
                    lost, gained = used[k], made[k]
                    olds.append((lost[i1, :], lost[i2, :], gained[q1, :], gained[q2, :]))
                for k, (i1, i2, q1, q2) in enumerate(places):
                    r = step * UNROLL + k0 + k
                    mix, old = mixes[k], olds[k]
                    used[k][i1, :] = old[0] - mix
                    used[k][i2, :] = old[1] - mix
                    made[k][q1, :] = old[2] + ylist[r] * mix
                    made[k][q2, :] = old[3] + ylist[listed + r] * mix

        def body(step, carry):
            some(step, UNROLL)
            return carry

        lax.fori_loop(0, real // UNROLL, body, 0)
        if real % UNROLL:
            some(real // UNROLL, real % UNROLL)

    def force(n):
        def body(p8, carry):
            at = sublane == p8
            for q in range(group // 8):
                r = chosen[q * 8 + p8]
                flux = held[n, at_flux + r // 8, pl.ds(r % 8, 1), :]
                value = jnp.where(at, flux, 0.0)
                i1, i2, q1, q2 = [
                    pl.ds(pl.multiple_of(ilist[row * listed + r] + q * 8, 8), 8) for row in range(4)
                ]
                lost, gained = used[q % BUFFERS], made[q % BUFFERS]
                one, two = lost[i1, :], lost[i2, :]
                three, four = gained[q1, :], gained[q2, :]
                lost[i1, :] = one - value
                lost[i2, :] = two - value
                gained[q1, :] = three + ylist[r] * value
                gained[q2, :] = four + ylist[listed + r] * value
            return carry

        lax.fori_loop(0, 8, body, 0)

    def total(at):
        value = used[0][at, :] + made[0][at, :]
        for k in range(1, BUFFERS):
            value = value + (used[k][at, :] + made[k][at, :])
        return value

    def each(work, target):
        def batch(step, count):
            places = [rows((step * 8 + k) * group) for k in range(count)]
            news = [work(place, step, k) for k, place in enumerate(places)]
            for place, (value, kept) in zip(places, news, strict=True):
                target[place, :] = value
                used[0][place, :] = kept

        def body(step, carry):
            batch(step, 8)
            return carry

        lax.fori_loop(0, species // 8, body, 0)
        if species % 8:
            batch(species // 8, species % 8)

    def substep(n, before):
        force(n)
        apply(before, n)

        def first(at, tile, k):
            right = total(at)
            value = right * held[n, at_fd + tile, k : k + 1, :]
            return value, used[0][at, :] + right * held[n, at_again + tile, k : k + 1, :]

        each(first, x)
        apply(x, n)

        def second(at, tile, k):
            right = total(at)
            value = before[at, :] + right * held[n, at_fda + tile, k : k + 1, :]
            return value, used[0][at, :] - right

        each(second, t)

    def more(n, carry):
        substep(n, t)
        return carry

    if origin is t:
        lax.fori_loop(start, stop, more, 0)
        return

    t[species * group :, :] = jnp.zeros((group, LANES), F32)

    @pl.when(start < stop)
    def _():
        substep(start, origin)
        lax.fori_loop(start + 1, stop, more, 0)

    @pl.when(start >= stop)
    def _():
        t[...] = origin[...]


def clear(refs):
    zero = jnp.zeros((LANES, LANES), F32)
    length = refs[0].shape[0]
    for at in range(0, length, LANES):
        for ref in refs:
            ref[at : min(at + LANES, length), :] = zero[0 : min(LANES, length - at)]


def weights(c):
    g = c * (1.0 - c * c) / 6.0
    up = c > 0
    half, square = 0.5 * c, 0.5 * c * c
    return (
        jnp.where(up, -g, 0.0),
        half + square + jnp.where(up, 3.0 * g, -g),
        1.0 - c * c + jnp.where(up, -3.0 * g, 3.0 * g),
        square - half + jnp.where(up, g, -3.0 * g),
        jnp.where(up, 0.0, g),
    )


def edge_kernel(
    chosen_in, reactants_in, products_in, yields_in, counts_in, permute_in, conc, rates, tangents,
    ilist_out, ylist_out, counts_out, conc_out, t, inner, other, s0, s1, s2, s3,
    raw, x, held, conc_in, rates_in, reactants, products, yields, counts, permute,
    pairs, columns, net_parts, hot, uses, base, chosen, ilist, ylist, *rest,
):
    sems = rest[-1]
    used, made = list(rest[:BUFFERS]), list(rest[BUFFERS : 2 * BUFFERS])
    species, real = conc.shape[0], rates.shape[0]
    group = tangents.shape[0]
    reactions = rates_in.shape[1]
    halves = conc_in.shape[0]
    starts, _ = rows_of(reactions, species)
    aligned = real // 8 * 8
    for half in range(halves):
        rates_in[half, aligned:] = jnp.zeros((reactions - aligned, LANES), F32)
    small = [
        pltpu.make_async_copy(conc.at[:, half, :], conc_in.at[half], sems.at[4])
        for half in range(halves)
    ] + [
        pltpu.make_async_copy(rates.at[:, half, :], rates_in.at[half, 0:real, :], sems.at[5])
        for half in range(halves)
    ]
    copies = tangent_copies(tangents, raw, sems)
    tiny = [
        pltpu.make_async_copy(source, target, sems.at[8])
        for source, target in (
            (chosen_in, chosen),
            (reactants_in, reactants),
            (products_in, products),
            (yields_in, yields),
            (counts_in, counts),
            (permute_in, permute),
        )
    ]
    for copy in tiny + small + copies:
        copy.start()
    clear([*used, *made])
    x[species * group :, :] = jnp.zeros((group, LANES), F32)
    for copy in tiny:
        copy.wait()

    pairs[...] = jnp.full(pairs.shape, -1, jnp.int32)
    pairs[0:2, 0:real] = reactants[...]
    pairs[2:4, 0:real] = products[...]
    columns[...] = jnp.zeros(columns.shape, F32)
    columns[0:2, 0:real] = yields[...]
    r0, r1, p0, p1 = [pairs[k : k + 1, :] for k in range(4)]
    y0, y1 = columns[0:1, :], columns[1:2, :]
    same, equal = r0 == r1, p0 == p1
    scale = jnp.where(same, 0.5, 1.0)
    parts = pairs.shape[1] // LANES
    ilist_out[...] = jnp.zeros(ilist_out.shape, jnp.int32)
    ylist_out[...] = jnp.zeros(ylist_out.shape, F32)
    for k, value in enumerate(
        (r0, jnp.where(same, species, r1), p0, jnp.where(equal, species, p1))
    ):
        value = jnp.where(r0 < 0, species, value) * group
        for part in range(parts):
            row = k * parts + part
            ilist_out[row : row + 1, :] = value[:, part * LANES : (part + 1) * LANES]
    for k, value in enumerate(
        (scale * (y0 + jnp.where(equal, y1, 0.0)), scale * jnp.where(equal, 0.0, y1))
    ):
        for part in range(parts):
            row = k * parts + part
            ylist_out[row : row + 1, :] = value[:, part * LANES : (part + 1) * LANES]
    lists = [
        pltpu.make_async_copy(source.at[row], target.at[pl.ds(row * LANES, LANES)], sems.at[6])
        for source, target, count in ((ilist_out, ilist, 4), (ylist_out, ylist, 2))
        for row in range(count * parts)
    ]
    for copy in lists:
        copy.start()

    row = lax.broadcasted_iota(jnp.int32, (species, reactions), 0)
    r0, r1, p0, p1 = [value[:, 0:reactions] for value in (r0, r1, p0, p1)]
    y0, y1 = y0[:, 0:reactions], y1[:, 0:reactions]
    uses_one = row == r0
    uses_two = row == r1
    net = (
        jnp.where(row == p0, y0, 0.0)
        + jnp.where(row == p1, y1, 0.0)
        - jnp.where(uses_one, 1.0, 0.0)
        - jnp.where(uses_two, 1.0, 0.0)
    )
    high, low = parts_of(net, 2)
    net_parts[0] = high
    net_parts[1] = low
    uses[0] = jnp.where(uses_one, 1.0, 0.0).astype(BF16)
    uses[1] = jnp.where(uses_two, 1.0, 0.0).astype(BF16)
    for k, value in enumerate((r0, r1)):
        change = (
            jnp.where(value == p0, y0, 0.0)
            + jnp.where(value == p1, y1, 0.0)
            - jnp.where(value == r0, 1.0, 0.0)
            - jnp.where(value == r1, 1.0, 0.0)
        )
        columns[k : k + 1, 0:reactions] = value.astype(F32)
        columns[2 + k : 3 + k, 0:reactions] = change
    turned = jnp.transpose(columns[...])[0:reactions]
    column = [turned[:, k : k + 1] for k in range(4)]
    lane = lane_of(reactions).astype(F32)
    for k in range(2):
        for at in range(0, species, LANES):
            width = min(LANES, species - at)
            value = jnp.where(column[k] == lane + float(at), 1.0, 0.0)[:, 0:width]
            hot[k * reactions : (k + 1) * reactions, at : at + width] = value.astype(BF16)
    same = column[0] == column[1]
    own_one, own_two = column[2], column[3]

    order = permute[...].astype(BF16)
    count = dot(jnp.broadcast_to(counts[...].astype(F32), (8, counts.shape[1])).astype(BF16), order)
    counts_out[...] = count
    count = count[0:1, :]
    factor = 1.0 / count
    highest = jnp.max(count).astype(jnp.int32)
    for copy in small:
        copy.wait()
    base[...] = select_right(jnp.concatenate([conc_in[0], conc_in[1]], axis=1), order, 3)
    rate = select_right(jnp.concatenate([rates_in[0], rates_in[1]], axis=1), order, 3)

    def keep(n, k, value):
        for ref, part in ((held, value[:, :LANES]), (other, value[:, LANES:])):
            full = value.shape[0] // 8 * 8
            first, tile = starts[k] // 8, (starts[k] + full) // 8
            ref[n, first:tile] = part[:full].reshape(full // 8, 8, LANES)
            if full < value.shape[0]:
                ref[n, tile, 0 : value.shape[0] - full, :] = part[full:]

    def substep(n, carry):
        c = base[...]
        picked = select_left(hot[...], c, 2)
        one, two = picked[:reactions], picked[reactions:]
        a = rate * two
        b = rate * one
        flux = a * one
        nets = (net_parts[0], net_parts[1])
        diagonal = select_left(uses[0], own_one * a, 2) + select_left(uses[1], own_two * b, 2)
        change = product(nets, flux)
        divisor = 1.0 - factor * diagonal
        fd = factor / divisor
        start = fd * change
        along = select_left(hot[...], start, 2)
        again = product(nets, a * along[:reactions] + b * along[reactions:])
        move = fd * (change + (again - diagonal * start))
        active = n.astype(F32) < count
        base[...] = c + jnp.where(active, move, 0.0)
        keep(n, 0, jnp.where(same, 2.0 * (a + b), a))
        keep(n, 1, jnp.where(same, 0.0, b))
        keep(n, 2, jnp.where(same, 2.0 * flux, flux))
        keep(n, 3, fd)
        keep(n, 4, jnp.where(active, fd, 0.0))
        keep(n, 5, fd * (count - 2.0 * diagonal) - 1.0)
        return carry

    lax.fori_loop(0, highest, substep, 0)
    conc_out[...] = base[...]

    for copy in copies:
        copy.wait()
    for q in range(raw.shape[1]):
        both = jnp.concatenate(
            [raw[:, q, half].reshape(species * 8, LANES) for half in range(halves)], axis=1
        )
        picked = select_right(both, order, 2)
        rows = slice(q * 8, (q + 1) * 8)
        for ref, part in ((t, picked[:, :LANES]), (inner, picked[:, LANES:])):
            by_species(ref, group)[0:species, rows, :] = part.reshape(species, 8, LANES)
    for ref in (t, inner):
        ref[species * group :, :] = jnp.zeros((group, LANES), F32)
    for copy in lists:
        copy.wait()
    own = jnp.max(count[:, :LANES]).astype(jnp.int32)
    tangent_chemistry(ilist, ylist, chosen, held, real, group, t, t, x, used, made, 0, own)

    rows = species * 8
    strips = swap_blocks(
        [
            by_species(t, group)[0:species, q * 8 : (q + 1) * 8, :].reshape(rows, LANES)
            for q in range(4)
        ]
    )
    quarter = up_to(-(-species // 4), 8)
    tails = []
    for q in range(4):
        part = base[q * quarter : min((q + 1) * quarter, species), 0:LANES]
        if part.shape[0] < quarter:
            empty = jnp.zeros((quarter - part.shape[0], LANES), F32)
            part = jnp.concatenate([part, empty], axis=0)
        tails.append(part)
    tails = swap_blocks(tails)
    even = even_row()
    strips[0:2] = ordered(even, strips[1], strips[0])
    tails[0:2] = ordered(even, tails[1], tails[0])
    for ref, value, last in zip((s0, s1, s2, s3), strips, tails, strict=True):
        ref[0:rows] = value
        ref[rows:] = last


def even_row():
    return (lax.axis_index("tile") // math.isqrt(lax.axis_size("tile"))) % 2 == 0


def even_tile():
    return lax.axis_index("tile") % 2 == 0


def ordered(even, one, two):
    return jnp.where(even, one, two), jnp.where(even, two, one)


def by_species(ref, group):
    return ref.reshape(ref.shape[0] // group, group, LANES)


def section(di, dj, c):
    value = jnp.zeros(di.shape, F32)
    for k, weight in enumerate(weights(c)):
        value = jnp.where((di == k - 2) & (dj == 0), weight, value)
    return value


def inner_kernel(
    real, ilist, ylist, chosen, counts, courant, side_pick, side_in, side_out, s0, s1, s2, s3,
    held, t_b,
    t, part, side_high, side_low,
    x, *rest,
):
    used, made = list(rest[:BUFFERS]), list(rest[BUFFERS : 2 * BUFFERS])
    group = chosen.shape[0]
    species = t_b.shape[0] // group - 1
    cx = jnp.concatenate([courant[0:1, :], courant[1:2, :]], axis=1)
    c = select_right(jnp.broadcast_to(cx, (8, cx.shape[1])), side_pick[...].astype(BF16), 3)[0:1, :]
    di = side_in[:, 0:1] - side_out[0:1, :]
    dj = side_in[:, 1:2] - side_out[1:2, :]
    map_ = jnp.where(side_in[:, 2:3] == side_out[2:3, :], section(di, dj, c), 0.0)
    high, low = parts_of(map_, 2)
    near = 4 * LANES
    side_high[...] = high[near:]
    side_low[...] = low[near:]
    last, first = ordered(even_row(), s0[...], s1[...])
    strips = jnp.concatenate([first, last, s2[...], s3[...]], axis=1)
    part[...] = product_right(strips, (high[:near], low[:near]))

    clear([*used, *made])
    x[species * group :, :] = jnp.zeros((group, LANES), F32)
    own = jnp.max(counts[0:1, LANES:]).astype(jnp.int32)
    tangent_chemistry(
        ilist, ylist, chosen, held, real, group, t_b, t, x, used, made,
        0, jnp.minimum(own, SPLIT),
    )


def side_kernel(part, one, two, side_high, side_low, to_one, to_two):
    east, west = ordered(even_row(), one[...], two[...])
    both = jnp.concatenate([west, east], axis=1)
    value = part[...] + product_right(both, (side_high[...], side_low[...]))
    to_one[...], to_two[...] = ordered(even_tile(), value[:, LANES:], value[:, :LANES])


def later_kernel(
    real, ilist, ylist, chosen, counts, held, t_b, courant, entries, cells, cells_rows,
    t, map_high, map_low,
    x, *rest,
):
    cx = jnp.concatenate([courant[0:1, :], courant[1:2, :]], axis=1)
    cy = jnp.concatenate([courant[2:3, :], courant[3:4, :]], axis=1)
    di = entries[:, 0:1] - cells_rows[0:1, :]
    dj = entries[:, 1:2] - cells_rows[1:2, :]
    along_x = section(di, dj, cx)
    late = lax.broadcasted_iota(jnp.int32, di.shape, 0) >= di.shape[0] - 64
    along_y = jnp.where(late, section(dj, di, cy), 0.0)
    both = section(cells[:, 1:2] - cells_rows[1:2, :], cells[:, 0:1] - cells_rows[0:1, :], cy)
    whole = along_y + jnp.dot(
        along_x, both, precision=lax.Precision.HIGHEST, preferred_element_type=F32
    )
    map_high[...], map_low[...] = parts_of(whole, 2)
    used, made = list(rest[:BUFFERS]), list(rest[BUFFERS : 2 * BUFFERS])
    group = chosen.shape[0]
    species = t_b.shape[0] // group - 1
    clear([*used, *made])
    x[species * group :, :] = jnp.zeros((group, LANES), F32)
    own = jnp.max(counts[0:1, LANES:]).astype(jnp.int32)
    tangent_chemistry(
        ilist, ylist, chosen, held, real, group, t_b, t, x, used, made,
        SPLIT, own,
    )


def advect_kernel(
    conc, h0, h1, h2, h3, map_high, map_low, t_a, t_b,
    t_out, conc_out,
    done, conc_done, halo_ref, sems,
):
    species = conc.shape[0]
    group = t_out.shape[0]
    rows = species * 8
    high, low = map_high[...], map_low[...]
    own = 2 * LANES
    local, outer = (high[:own], low[:own]), (high[own:], low[own:])

    east, west = ordered(even_row(), h0[...], h1[...])
    north, south = ordered(even_tile(), h2[...], h3[...])
    halo = swap_blocks([west, east, south, north])
    twice = jnp.concatenate([outer[0], outer[0]], axis=0)

    def from_halo(value):
        high, low = parts_of(value, 2)
        return dot(jnp.concatenate([high, low], axis=1), twice) + dot(high, outer[1])

    outside = jnp.concatenate([value[rows:] for value in halo], axis=0)
    base = product_right(conc[...], local) + from_halo(outside[0:species])
    copies = []
    for half in range(2):
        conc_done[half] = base[:, half * LANES : (half + 1) * LANES]
        copies.append(
            pltpu.make_async_copy(conc_done.at[half], conc_out.at[:, half, :], sems.at[1])
        )
        copies[-1].start()
    for q in range(4):
        halo_ref[q] = halo[q][0:rows]

    def sent(q):
        return [
            pltpu.make_async_copy(done.at[:, q, :, p8, :], t_out.at[q * 8 + p8], sems.at[0])
            for p8 in range(8)
        ]

    def body(q, carry):
        part = pl.ds(pl.multiple_of(q * 8, 8), 8)
        inside = jnp.concatenate(
            [by_species(ref, group)[0:species, part, :].reshape(rows, LANES) for ref in (t_a, t_b)],
            axis=1,
        )
        value = product_right(inside, local) + from_halo(halo_ref[q])
        for half in range(2):
            done[:, q, half] = value[:, half * LANES : (half + 1) * LANES].reshape(
                species, 8, LANES
            )
        for copy in sent(q):
            copy.start()
        return carry

    lax.fori_loop(0, group // 8, body, 0)
    for q in range(group // 8):
        copies += sent(q)
    for copy in copies:
        copy.wait()


def exchanged(value, by, odd):
    size = lax.axis_size("tile")
    pairs = [(i, i + by) for i in range(size - by) if (i // by) % 2 == odd]
    return lax.ppermute(value, "tile", pairs + [(j, i) for i, j in pairs])


def per_device(
    concentrations, tangents, rates, substeps, courant, reactants, products, yields, reaction_index
):
    species = concentrations.shape[0]
    cells = CX * CY
    halves = cells // LANES
    group = tangents.shape[0]
    real = rates.shape[0]
    reactions = up_to(real, 8)
    listed = up_to(reactions, LANES)
    lists = up_to(4 * listed // LANES, 8)
    across = math.isqrt(lax.axis_size("tile"))
    table = static_tables()
    vmem = pl.BlockSpec(memory_space=pltpu.VMEM)
    smem = pl.BlockSpec(memory_space=pltpu.SMEM)
    hbm = pl.BlockSpec(memory_space=pltpu.HBM)
    limit = pltpu.CompilerParams(vmem_limit_bytes=VMEM_LIMIT)
    _, held_rows = rows_of(reactions, species)

    def shape(*sizes, dtype=F32):
        return jax.ShapeDtypeStruct(sizes, dtype)

    conc = concentrations.reshape(species, halves, LANES)
    sens = tangents.reshape(group, species, halves, LANES)
    rate_rows = rates.reshape(real, halves, LANES)
    numbers = courant.reshape(2 * halves, LANES)

    state = shape((species + 1) * group, LANES)
    strip = shape(species * 8 + up_to(-(-species // 4), 8), LANES)
    wide = shape(strip.shape[0], 2 * LANES)
    held = shape(NMAX, held_rows // 8, 8, LANES)
    work = [pltpu.VMEM(state.shape, F32)] * (1 + 2 * BUFFERS)
    raw = pltpu.VMEM((species, group // 8, halves, 8, LANES), F32)

    ilist, ylist, counts, conc_end, t_a, t_b, held_b, s0, s1, s2, s3 = pl.pallas_call(
        edge_kernel,
        out_shape=[
            shape(lists, LANES, dtype=jnp.int32),
            shape(lists, LANES),
            shape(8, cells),
            shape(species, cells),
            state,
            state,
            held,
            *([strip] * 4),
        ],
        in_specs=[hbm] * 9,
        out_specs=[vmem] * 11,
        scratch_shapes=[
            raw,
            work[0],
            pltpu.VMEM(held.shape, F32),
            pltpu.VMEM((halves, species, LANES), F32),
            pltpu.VMEM((halves, reactions, LANES), F32),
            pltpu.VMEM((2, real), jnp.int32),
            pltpu.VMEM((2, real), jnp.int32),
            pltpu.VMEM((2, real), F32),
            pltpu.VMEM((1, cells), jnp.int32),
            pltpu.VMEM((cells, cells), F32),
            pltpu.VMEM((8, listed), jnp.int32),
            pltpu.VMEM((LANES, listed), F32),
            pltpu.VMEM((2, species, reactions), BF16),
            pltpu.VMEM((2 * reactions, species), BF16),
            pltpu.VMEM((2, species, reactions), BF16),
            pltpu.VMEM((species, cells), F32),
            pltpu.SMEM((group,), jnp.int32),
            pltpu.SMEM((4 * listed,), jnp.int32),
            pltpu.SMEM((2 * listed,), F32),
            *work[1:],
            pltpu.SemaphoreType.DMA((9,)),
        ],
        compiler_params=limit,
        name="edge_columns",
    )(
        *[
            pltpu.with_memory_space_constraint(value, pltpu.HBM)
            for value in (
                reaction_index, reactants.T, products.T, yields.T, substeps,
                jnp.asarray(table["permute"]), conc, rate_rows, sens,
            )
        ]
    )

    ilist, ylist = ilist.reshape(-1)[: 4 * listed], ylist.reshape(-1)
    x_one = exchanged(s0, across, 0)
    x_two = exchanged(s1, across, 1)

    t_b, part, side_high, side_low = pl.pallas_call(
        functools.partial(inner_kernel, real),
        out_shape=[state, wide] + [shape(2 * LANES, 2 * LANES, dtype=BF16)] * 2,
        in_specs=[smem] * 3 + [vmem] * 11,
        out_specs=[vmem] * 4,
        scratch_shapes=work,
        compiler_params=limit,
        name="inner_columns",
    )(
        ilist, ylist, reaction_index, counts, numbers, jnp.asarray(table["side_pick"]),
        jnp.asarray(table["side_in"]), jnp.asarray(table["side_out"]), s0, s1, s2, s3,
        held_b, t_b,
    )

    to_one, to_two = pl.pallas_call(
        side_kernel,
        out_shape=[strip, strip],
        in_specs=[vmem] * 5,
        out_specs=[vmem] * 2,
        compiler_params=limit,
        name="y_edges",
    )(part, x_one, x_two, side_high, side_low)
    y_one = exchanged(to_one, 1, 0)
    y_two = exchanged(to_two, 1, 1)

    map_ = shape(3 * LANES, cells, dtype=BF16)
    t_b, map_high, map_low = pl.pallas_call(
        functools.partial(later_kernel, real),
        out_shape=[state, map_, map_],
        in_specs=[smem] * 3 + [vmem] * 7,
        out_specs=[vmem] * 3,
        scratch_shapes=work,
        compiler_params=limit,
        name="inner_later",
    )(
        ilist, ylist, reaction_index, counts, held_b, t_b, numbers,
        jnp.asarray(table["entries"]), jnp.asarray(table["cells"]),
        jnp.asarray(table["cells_rows"]),
    )

    result, conc_out = pl.pallas_call(
        advect_kernel,
        out_shape=[shape(group, species, halves, LANES), shape(species, halves, LANES)],
        in_specs=[vmem] * 9,
        out_specs=[hbm, hbm],
        scratch_shapes=[
            raw,
            pltpu.VMEM((halves, species, LANES), F32),
            pltpu.VMEM((group // 8, species * 8, LANES), F32),
            pltpu.SemaphoreType.DMA((2,)),
        ],
        compiler_params=limit,
        name="advection",
    )(
        conc_end, x_one, x_two, y_one, y_two, map_high, map_low, t_a, t_b,
    )
    return (
        conc_out.reshape(species, 1, cells),
        result.reshape(group, species, 1, cells),
    )


def solution(mesh):
    in_specs = (
        P(None, "tile", None),
        P("pgrp", None, "tile", None),
        P(None, "tile", None),
        P("tile", None),
        P(None, "tile", None),
        P(),
        P(),
        P(),
        P("pgrp"),
    )
    out_specs = (P(None, "tile", None), P("pgrp", None, "tile", None))
    return jax.shard_map(
        per_device, mesh=mesh, in_specs=in_specs, out_specs=out_specs, check_vma=False
    )
```

profile of v0, /device:TPU:13, one launch (start us, length us, event | category | flops | bytes accessed | tf_op | source)
XLA Modules:
  0.0 69.1 jit_solution(16590654012243645684)
XLA Ops:
  0.6 0.0 copy-start
  0.6 0.0 copy-start.1
  0.7 0.0 copy-start.4
  0.7 0.0 copy-start.5
  0.7 0.0 copy-start.6
  0.7 27.9 %edge_columns.1 = (s32[8,128]{1,0:T(8,128)S(1)}, f32[8,128]{1,0:T(8,128)S(1)}, f32[8,256]{1,0:T(8,128)S(1)}, f32[130,256]{1,0:T(8,128)S(1)}, f32[4192,128]{1,0:T...) custom-call(s32[32]{0:T(128)} %chosen.3, ...), custom_call_target="tpu_custom_call" | custom-call | tf_op jit(solution)/shard_map/edge_columns/pallas_call | solution.py:685
  28.6 0.1 collective-permute-start
  28.6 3.2 %collective-permute-start.1 = (f32[1080,128]{1,0:T(8,128)S(1)}, f32[1080,128]{1,0:T(8,128)S(1)}, u32[]{:S(2)}, u32[]{:S(2)}) collective-permute-start(f32[1080,128]{1,0:T(8,128)S(1)} %get-tuple-element.26.s1), channel_id=1, source_target_pairs={{8,16},{10,18},{12,20},{14,22},{16,8},{18,10},{20,12},{22,14},{9,1... | collective-permute-start | bytes 1658888 | tf_op jit(solution)/shard_map/ppermute | solution.py:648
  31.8 0.0 copy-done
  31.9 0.0 copy-done.1
  31.9 0.0 copy-done.4
  31.9 0.0 copy-done.5
  31.9 0.0 copy-done.6
  31.9 12.2 %inner_columns.1 = (f32[4192,128]{1,0:T(8,128)S(1)}, f32[1080,256]{1,0:T(8,128)S(1)}, bf16[256,256]{1,0:T(8,128)(2,1)S(1)}, bf16[256,256]{1,0:T(8,128)(2,1)S(1)}) custom-call(s32[1024]{0:T(1024)S(1)} %bitcast.11, f32[1024]{0:T(1024)S(1)} %bitcast.13, s32[32]{0:T(128)S(1)} %copy-done.5, f32[8,256]{1,0:T(8,128)S(1)} %get-tuple-element.29.counts, ...), custom_call_target="tpu_custom_call" | custom-call | tf_op jit(solution)/shard_map/inner_columns/pallas_call | solution.py:738
  44.1 0.0 copy-start.2
  44.1 0.0 copy-start.3
  44.1 0.0 copy-start.7
  44.1 0.0 collective-permute-done.one.h0
  44.1 0.0 collective-permute-done.1.two.h1
  44.1 0.6 y_edges.1
  44.8 1.4 %collective-permute-start.2 = (f32[1080,128]{1,0:T(8,128)S(1)}, f32[1080,128]{1,0:T(8,128)S(1)}, u32[]{:S(2)}, u32[]{:S(2)}) collective-permute-start(f32[1080,128]{1,0:T(8,128)S(1)} %get-tuple-element.37), channel_id=1, source_target_pairs={{0,2},{4,6},{8,10},{12,14},{16,18},{20,22},{24,26},{28,30},{2,0},{... | collective-permute-start | bytes 1658888 | tf_op jit(solution)/shard_map/ppermute | solution.py:648
  46.2 4.4 %collective-permute-start.3 = (f32[1080,128]{1,0:T(8,128)S(1)}, f32[1080,128]{1,0:T(8,128)S(1)}, u32[]{:S(2)}, u32[]{:S(2)}) collective-permute-start(f32[1080,128]{1,0:T(8,128)S(1)} %get-tuple-element.38), channel_id=1, source_target_pairs={{2,4},{6,8},{10,12},{14,16},{18,20},{22,24},{26,28},{4,2},{8,6},{1... | collective-permute-start | bytes 1658888 | tf_op jit(solution)/shard_map/ppermute | solution.py:648
  50.5 0.0 copy-done.2
  50.6 0.0 copy-done.3
  50.6 0.0 copy-done.7
  50.6 11.2 %inner_later.1 = (f32[4192,128]{1,0:T(8,128)S(1)}, bf16[384,256]{1,0:T(8,128)(2,1)S(1)}, bf16[384,256]{1,0:T(8,128)(2,1)S(1)}) custom-call(s32[1024]{0:T(1024)S(1)} %bitcast.12, f32[1024]{0:T(1024)S(1)} %bitcast.14, s32[32]{0:T(128)S(1)} %copy-done.5, f32[8,256]{1,0:T(8,128)S(1)} %get-tuple-element.29.counts, f32[4,135,8,128]{3,2,1,0:T(8,128)S(1)} %get-tuple-element.32.held, ...), custom_call_target="tpu_custom_call" | custom-call | tf_op jit(solution)/shard_map/inner_later/pallas_call | solution.py:764
  61.8 0.0 collective-permute-done.2.h2
  61.8 1.4 %collective-permute-done.3.h3 = f32[1080,128]{1,0:T(8,128)S(1)} collective-permute-done((f32[1080,128]{1,0:T(8,128)S(1)}, f32[1080,128]{1,0:T(8,128)S(1)}, u32[]{:S(2)}, u32[]{:S(2)}) %collective-permute-start.3) | collective-permute-done | bytes 552992 | tf_op jit(solution)/shard_map/ppermute | solution.py:648
  63.1 5.8 %advection.1 = (f32[32,130,2,128]{3,2,1,0:T(2,128)}, f32[130,2,128]{2,1,0:T(2,128)}) custom-call(f32[130,256]{1,0:T(8,128)S(1)} %get-tuple-element.24.conc, f32[1080,128]{1,0:T(8,128)S(1)} %collective-permute-done.one.h0, f32[1080,128]{1,0:T(8,128)S(1)} %collective-permute-done.1.two.h1, f32[1080,128]{1,0:T(8,128)S(1)} %collective-permute-done.2.h2, ...), custom_call_target="tpu_custom_call" | custom-call | tf_op jit(solution)/shard_map/advection/pallas_call | solution.py:778
Async XLA Ops:
  0.6 31.2 %copy-start = (s32[768,3]{1,0:T(8,128)S(1)}, s32[768,3]{1,0:T(8,128)}, u32[]{:S(2)}) copy-start(s32[768,3]{1,0:T(8,128)} %constant.16.clone.side_in) | copy-start | bytes 27652
  0.6 31.2 %copy-start.1 = (f32[256,256]{1,0:T(8,128)S(1)}, f32[256,256]{1,0:T(8,128)}, u32[]{:S(2)}) copy-start(f32[256,256]{1,0:T(8,128)} %constant.15.clone.side_pick) | copy-start | bytes 786436
  0.7 31.2 %copy-start.4 = (f32[2,1,256]{2,1,0:T(1,128)S(1)}, f32[2,1,256]{2,1,0:T(1,128)}, u32[]{:S(2)}) copy-start(f32[2,1,256]{2,1,0:T(1,128)} %param.20) | copy-start | bytes 6148
  0.7 31.2 %copy-start.5 = (s32[32]{0:T(128)S(1)}, s32[32]{0:T(128)}, u32[]{:S(2)}) copy-start(s32[32]{0:T(128)} %chosen.3) | copy-start | bytes 388
  0.7 31.2 %copy-start.6 = (s32[3,256]{1,0:T(4,128)S(1)}, s32[3,256]{1,0:T(4,128)}, u32[]{:S(2)}) copy-start(s32[3,256]{1,0:T(4,128)} %constant.17.clone.side_out) | copy-start | bytes 9220
  28.6 15.6 %collective-permute-start = (f32[1080,128]{1,0:T(8,128)S(1)}, f32[1080,128]{1,0:T(8,128)S(1)}, u32[]{:S(2)}, u32[]{:S(2)}) collective-permute-start(f32[1080,128]{1,0:T(8,128)S(1)} %get-tuple-element.25.s0), channel_id=1, source_target_pairs={{0,8},{2,10},{4,12},{6,14},{16,24},{18,26},{20,28},{22,30},{8,0},{... | collective-permute-start | bytes 1658888 | tf_op jit(solution)/shard_map/ppermute | solution.py:648
  28.6 15.5 %collective-permute-start.1 = (f32[1080,128]{1,0:T(8,128)S(1)}, f32[1080,128]{1,0:T(8,128)S(1)}, u32[]{:S(2)}, u32[]{:S(2)}) collective-permute-start(f32[1080,128]{1,0:T(8,128)S(1)} %get-tuple-element.26.s1), channel_id=1, source_target_pairs={{8,16},{10,18},{12,20},{14,22},{16,8},{18,10},{20,12},{22,14},{9,1... | collective-permute-start | bytes 1658888 | tf_op jit(solution)/shard_map/ppermute | solution.py:648
  44.1 6.5 %copy-start.2 = (s32[384,2]{1,0:T(8,128)S(1)}, s32[384,2]{1,0:T(8,128)}, u32[]{:S(2)}) copy-start(s32[384,2]{1,0:T(8,128)} %constant.18.clone.entries) | copy-start | bytes 9220
  44.1 6.5 %copy-start.3 = (s32[256,2]{1,0:T(8,128)S(1)}, s32[256,2]{1,0:T(8,128)}, u32[]{:S(2)}) copy-start(s32[256,2]{1,0:T(8,128)} %constant.19.clone.cells) | copy-start | bytes 6148
  44.1 6.5 %copy-start.7 = (s32[2,256]{1,0:T(2,128)S(1)}, s32[2,256]{1,0:T(2,128)}, u32[]{:S(2)}) copy-start(s32[2,256]{1,0:T(2,128)} %constant.20.clone.cells_rows) | copy-start | bytes 6148
  44.8 17.0 %collective-permute-start.2 = (f32[1080,128]{1,0:T(8,128)S(1)}, f32[1080,128]{1,0:T(8,128)S(1)}, u32[]{:S(2)}, u32[]{:S(2)}) collective-permute-start(f32[1080,128]{1,0:T(8,128)S(1)} %get-tuple-element.37), channel_id=1, source_target_pairs={{0,2},{4,6},{8,10},{12,14},{16,18},{20,22},{24,26},{28,30},{2,0},{... | collective-permute-start | bytes 1658888 | tf_op jit(solution)/shard_map/ppermute | solution.py:648
  46.2 17.0 %collective-permute-start.3 = (f32[1080,128]{1,0:T(8,128)S(1)}, f32[1080,128]{1,0:T(8,128)S(1)}, u32[]{:S(2)}, u32[]{:S(2)}) collective-permute-start(f32[1080,128]{1,0:T(8,128)S(1)} %get-tuple-element.38), channel_id=1, source_target_pairs={{2,4},{6,8},{10,12},{14,16},{18,20},{22,24},{26,28},{4,2},{8,6},{1... | collective-permute-start | bytes 1658888 | tf_op jit(solution)/shard_map/ppermute | solution.py:648
where the time goes:
time: 69.8 us; the launch traced here: 69.1 us
  Pallas kernels  57.7 us (83%)
  starting transfers between devices  9.04 us (13%)
  waiting for transfers between devices  1.37 us (2%)
  between operations  1 us (1%)
    pallas_call x1, Pallas kernels, per_device(): pl.pallas_call(edge_kernel, out_shape=[shape(lists, LANES, dtype=jnp.int3...  27.9 us
    pallas_call x1, Pallas kernels, per_device(): pl.pallas_call(functools.partial(inner_kernel, real), out_shape=[state, w...  12.2 us
    pallas_call x1, Pallas kernels, per_device(): pl.pallas_call(functools.partial(later_kernel, real), out_shape=[state, m...  11.2 us
    ppermute x4, starting transfers between devices, exchanged(): return lax.ppermute(value, 'tile', pairs + [(j, i) for i, j in pairs])  9.04 us
    pallas_call x1, Pallas kernels, per_device(): pl.pallas_call(advect_kernel, out_shape=[shape(group, species, halves, LA...  5.82 us
  transfers between devices with their start and end apart: 4, of which 1 were waited for; matrix products, arithmetic and copies ran while one was open for 0% of the time, Pallas kernels for 34%

commit v1 on v0

--- a/solution.py
+++ b/solution.py
@@ -207,7 +207,7 @@
                 gained[q2, :] = four + ylist[listed + r] * value
             return carry
 
-        lax.fori_loop(0, 8, body, 0)
+        lax.fori_loop(0, 8, body, 0, unroll=4)
 
     def total(at):
         value = used[0][at, :] + made[0][at, :]
@@ -582,7 +582,7 @@
 
 
 def advect_kernel(
-    conc, h0, h1, h2, h3, map_high, map_low, t_a, t_b,
+    conc, h0, h1, h3, h2, map_high, map_low, t_a, t_b,
     t_out, conc_out,
     done, conc_done, halo_ref, sems,
 ):
@@ -757,8 +757,8 @@
         compiler_params=limit,
         name="y_edges",
     )(part, x_one, x_two, side_high, side_low)
+    y_two = exchanged(to_two, 1, 1)
     y_one = exchanged(to_one, 1, 0)
-    y_two = exchanged(to_two, 1, 1)
 
     map_ = shape(3 * LANES, cells, dtype=BF16)
     t_b, map_high, map_low = pl.pallas_call(
@@ -789,7 +789,7 @@
         compiler_params=limit,
         name="advection",
     )(
-        conc_end, x_one, x_two, y_one, y_two, map_high, map_low, t_a, t_b,
+        conc_end, x_one, x_two, y_two, y_one, map_high, map_low, t_a, t_b,
     )
     return (
         conc_out.reshape(species, 1, cells),

time: 69.8 us -> 67.7 us (0.970); the launches traced: 69.1 us -> 68.5 us
  Pallas kernels: 57.7 us -> 37 us
  starting transfers between devices: 9.04 us -> 20.7 us
  waiting for transfers between devices: 1.37 us -> 9.79 us
    pallas_call x1, Pallas kernels: 27.9 us -> 16.1 us  [per_device(): pl.pallas_call(edge_kernel, out_shape=[shape(lists, LANES, dtype=jnp.int3...]
    ppermute x4, starting transfers between devices: 9.04 us -> 20.7 us  [exchanged(): return lax.ppermute(value, 'tile', pairs + [(j, i) for i, j in pairs])]
    pallas_call x1, Pallas kernels: 11.2 us -> 2.28 us  [per_device(): pl.pallas_call(functools.partial(later_kernel, real), out_shape=[state, m...]
    ppermute x4, waiting for transfers between devices: 1.37 us -> 9.79 us  [exchanged(): return lax.ppermute(value, 'tile', pairs + [(j, i) for i, j in pairs])]
  transfers between devices with their start and end apart: 4 -> 4, of which waited for: 1 -> 1; matrix products, arithmetic and copies ran while one was open for 0% -> 0% of each run, Pallas kernels for 34% -> 21%
where the time goes in v1:
time: 67.7 us; the launch traced here: 68.5 us
  Pallas kernels  37 us (55%)
  starting transfers between devices  20.7 us (31%)
  waiting for transfers between devices  9.79 us (14%)
  between operations  1 us (1%)
    ppermute x4, starting transfers between devices, exchanged(): return lax.ppermute(value, 'tile', pairs + [(j, i) for i, j in pairs])  20.7 us
    pallas_call x1, Pallas kernels, per_device(): pl.pallas_call(edge_kernel, out_shape=[shape(lists, LANES, dtype=jnp.int3...  16.1 us
    pallas_call x1, Pallas kernels, per_device(): pl.pallas_call(functools.partial(inner_kernel, real), out_shape=[state, w...  12.1 us
    ppermute x4, waiting for transfers between devices, exchanged(): return lax.ppermute(value, 'tile', pairs + [(j, i) for i, j in pairs])  9.79 us
    pallas_call x1, Pallas kernels, per_device(): pl.pallas_call(advect_kernel, out_shape=[shape(group, species, halves, LA...  5.82 us
    pallas_call x1, Pallas kernels, per_device(): pl.pallas_call(functools.partial(later_kernel, real), out_shape=[state, m...  2.28 us
  transfers between devices with their start and end apart: 4, of which 1 were waited for; matrix products, arithmetic and copies ran while one was open for 0% of the time, Pallas kernels for 21%

profile of v1, /device:TPU:13, one launch (start us, length us, event | category | flops | bytes accessed | tf_op | source)
XLA Modules:
  0.0 68.5 jit_solution(6814058404248262908)
XLA Ops:
  0.6 0.0 copy-start
  0.6 0.0 copy-start.1
  0.7 0.0 copy-start.4
  0.7 0.0 copy-start.5
  0.7 0.0 copy-start.6
  0.7 16.1 %edge_columns.1 = (s32[8,128]{1,0:T(8,128)S(1)}, f32[8,128]{1,0:T(8,128)S(1)}, f32[8,256]{1,0:T(8,128)S(1)}, f32[130,256]{1,0:T(8,128)S(1)}, f32[4192,128]{1,0:T...) custom-call(s32[32]{0:T(128)} %chosen.3, ...), custom_call_target="tpu_custom_call" | custom-call | tf_op jit(solution)/shard_map/edge_columns/pallas_call | solution.py:685
  16.8 0.1 collective-permute-start
  16.9 3.2 %collective-permute-start.1 = (f32[1080,128]{1,0:T(8,128)S(1)}, f32[1080,128]{1,0:T(8,128)S(1)}, u32[]{:S(2)}, u32[]{:S(2)}) collective-permute-start(f32[1080,128]{1,0:T(8,128)S(1)} %get-tuple-element.26.s1), channel_id=1, source_target_pairs={{8,16},{10,18},{12,20},{14,22},{16,8},{18,10},{20,12},{22,14},{9,1... | collective-permute-start | bytes 1658888 | tf_op jit(solution)/shard_map/ppermute | solution.py:648
  20.1 0.0 copy-done
  20.1 0.0 copy-done.1
  20.1 0.0 copy-done.4
  20.1 0.0 copy-done.5
  20.2 0.0 copy-done.6
  20.2 12.1 %inner_columns.1 = (f32[4192,128]{1,0:T(8,128)S(1)}, f32[1080,256]{1,0:T(8,128)S(1)}, bf16[256,256]{1,0:T(8,128)(2,1)S(1)}, bf16[256,256]{1,0:T(8,128)(2,1)S(1)}) custom-call(s32[1024]{0:T(1024)S(1)} %bitcast.11, f32[1024]{0:T(1024)S(1)} %bitcast.13, s32[32]{0:T(128)S(1)} %copy-done.5, f32[8,256]{1,0:T(8,128)S(1)} %get-tuple-element.29.counts, ...), custom_call_target="tpu_custom_call" | custom-call | tf_op jit(solution)/shard_map/inner_columns/pallas_call | solution.py:738
  32.3 0.0 copy-start.2
  32.3 0.0 copy-start.3
  32.3 0.0 copy-start.7
  32.3 0.0 collective-permute-done.one.h0
  32.3 0.0 collective-permute-done.1.two.h1
  32.3 0.6 y_edges.1
  33.0 17.3 %collective-permute-start.2 = (f32[1080,128]{1,0:T(8,128)S(1)}, f32[1080,128]{1,0:T(8,128)S(1)}, u32[]{:S(2)}, u32[]{:S(2)}) collective-permute-start(f32[1080,128]{1,0:T(8,128)S(1)} %get-tuple-element.37), channel_id=1, source_target_pairs={{2,4},{6,8},{10,12},{14,16},{18,20},{22,24},{26,28},{4,2},{8,6},{1... | collective-permute-start | bytes 1658888 | tf_op jit(solution)/shard_map/ppermute | solution.py:648
  50.3 0.1 collective-permute-start.3
  50.4 0.0 copy-done.2
  50.4 0.0 copy-done.3
  50.4 0.0 copy-done.7
  50.4 2.3 %inner_later.1 = (f32[4192,128]{1,0:T(8,128)S(1)}, bf16[384,256]{1,0:T(8,128)(2,1)S(1)}, bf16[384,256]{1,0:T(8,128)(2,1)S(1)}) custom-call(s32[1024]{0:T(1024)S(1)} %bitcast.12, f32[1024]{0:T(1024)S(1)} %bitcast.14, s32[32]{0:T(128)S(1)} %copy-done.5, f32[8,256]{1,0:T(8,128)S(1)} %get-tuple-element.29.counts, f32[4,135,8,128]{3,2,1,0:T(8,128)S(1)} %get-tuple-element.32.held, ...), custom_call_target="tpu_custom_call" | custom-call | tf_op jit(solution)/shard_map/inner_later/pallas_call | solution.py:764
  52.7 9.8 %collective-permute-done.2.h3 = f32[1080,128]{1,0:T(8,128)S(1)} collective-permute-done((f32[1080,128]{1,0:T(8,128)S(1)}, f32[1080,128]{1,0:T(8,128)S(1)}, u32[]{:S(2)}, u32[]{:S(2)}) %collective-permute-start.2) | collective-permute-done | bytes 552992 | tf_op jit(solution)/shard_map/ppermute | solution.py:648
  62.5 0.0 collective-permute-done.3.h2
  62.5 5.8 %advection.1 = (f32[32,130,2,128]{3,2,1,0:T(2,128)}, f32[130,2,128]{2,1,0:T(2,128)}) custom-call(f32[130,256]{1,0:T(8,128)S(1)} %get-tuple-element.24.conc, f32[1080,128]{1,0:T(8,128)S(1)} %collective-permute-done.one.h0, f32[1080,128]{1,0:T(8,128)S(1)} %collective-permute-done.1.two.h1, f32[1080,128]{1,0:T(8,128)S(1)} %collective-permute-done.2.h3, ...), custom_call_target="tpu_custom_call" | custom-call | tf_op jit(solution)/shard_map/advection/pallas_call | solution.py:778
Async XLA Ops:
  0.6 19.5 %copy-start = (s32[768,3]{1,0:T(8,128)S(1)}, s32[768,3]{1,0:T(8,128)}, u32[]{:S(2)}) copy-start(s32[768,3]{1,0:T(8,128)} %constant.16.clone.side_in) | copy-start | bytes 27652
  0.6 19.5 %copy-start.1 = (f32[256,256]{1,0:T(8,128)S(1)}, f32[256,256]{1,0:T(8,128)}, u32[]{:S(2)}) copy-start(f32[256,256]{1,0:T(8,128)} %constant.15.clone.side_pick) | copy-start | bytes 786436
  0.7 19.5 %copy-start.4 = (f32[2,1,256]{2,1,0:T(1,128)S(1)}, f32[2,1,256]{2,1,0:T(1,128)}, u32[]{:S(2)}) copy-start(f32[2,1,256]{2,1,0:T(1,128)} %param.20) | copy-start | bytes 6148
  0.7 19.5 %copy-start.5 = (s32[32]{0:T(128)S(1)}, s32[32]{0:T(128)}, u32[]{:S(2)}) copy-start(s32[32]{0:T(128)} %chosen.3) | copy-start | bytes 388
  0.7 19.5 %copy-start.6 = (s32[3,256]{1,0:T(4,128)S(1)}, s32[3,256]{1,0:T(4,128)}, u32[]{:S(2)}) copy-start(s32[3,256]{1,0:T(4,128)} %constant.17.clone.side_out) | copy-start | bytes 9220
  16.8 15.5 %collective-permute-start = (f32[1080,128]{1,0:T(8,128)S(1)}, f32[1080,128]{1,0:T(8,128)S(1)}, u32[]{:S(2)}, u32[]{:S(2)}) collective-permute-start(f32[1080,128]{1,0:T(8,128)S(1)} %get-tuple-element.25.s0), channel_id=1, source_target_pairs={{0,8},{2,10},{4,12},{6,14},{16,24},{18,26},{20,28},{22,30},{8,0},{... | collective-permute-start | bytes 1658888 | tf_op jit(solution)/shard_map/ppermute | solution.py:648
  16.9 15.4 %collective-permute-start.1 = (f32[1080,128]{1,0:T(8,128)S(1)}, f32[1080,128]{1,0:T(8,128)S(1)}, u32[]{:S(2)}, u32[]{:S(2)}) collective-permute-start(f32[1080,128]{1,0:T(8,128)S(1)} %get-tuple-element.26.s1), channel_id=1, source_target_pairs={{8,16},{10,18},{12,20},{14,22},{16,8},{18,10},{20,12},{22,14},{9,1... | collective-permute-start | bytes 1658888 | tf_op jit(solution)/shard_map/ppermute | solution.py:648
  32.3 18.1 %copy-start.2 = (s32[384,2]{1,0:T(8,128)S(1)}, s32[384,2]{1,0:T(8,128)}, u32[]{:S(2)}) copy-start(s32[384,2]{1,0:T(8,128)} %constant.18.clone.entries) | copy-start | bytes 9220
  32.3 18.1 %copy-start.3 = (s32[256,2]{1,0:T(8,128)S(1)}, s32[256,2]{1,0:T(8,128)}, u32[]{:S(2)}) copy-start(s32[256,2]{1,0:T(8,128)} %constant.19.clone.cells) | copy-start | bytes 6148
  32.3 18.1 %copy-start.7 = (s32[2,256]{1,0:T(2,128)S(1)}, s32[2,256]{1,0:T(2,128)}, u32[]{:S(2)}) copy-start(s32[2,256]{1,0:T(2,128)} %constant.20.clone.cells_rows) | copy-start | bytes 6148
  33.0 29.5 %collective-permute-start.2 = (f32[1080,128]{1,0:T(8,128)S(1)}, f32[1080,128]{1,0:T(8,128)S(1)}, u32[]{:S(2)}, u32[]{:S(2)}) collective-permute-start(f32[1080,128]{1,0:T(8,128)S(1)} %get-tuple-element.37), channel_id=1, source_target_pairs={{2,4},{6,8},{10,12},{14,16},{18,20},{22,24},{26,28},{4,2},{8,6},{1... | collective-permute-start | bytes 1658888 | tf_op jit(solution)/shard_map/ppermute | solution.py:648
  50.3 12.2 %collective-permute-start.3 = (f32[1080,128]{1,0:T(8,128)S(1)}, f32[1080,128]{1,0:T(8,128)S(1)}, u32[]{:S(2)}, u32[]{:S(2)}) collective-permute-start(f32[1080,128]{1,0:T(8,128)S(1)} %get-tuple-element.38), channel_id=1, source_target_pairs={{0,2},{4,6},{8,10},{12,14},{16,18},{20,22},{24,26},{28,30},{2,0},{... | collective-permute-start | bytes 1658888 | tf_op jit(solution)/shard_map/ppermute | solution.py:648

commit v2 on v1

--- a/solution.py
+++ b/solution.py
@@ -227,7 +227,7 @@
             batch(step, 8)
             return carry
 
-        lax.fori_loop(0, species // 8, body, 0)
+        lax.fori_loop(0, species // 8, body, 0, unroll=2)
         if species % 8:
             batch(species // 8, species % 8)
 
@@ -429,7 +429,8 @@
         b = rate * one
         flux = a * one
         nets = (net_parts[0], net_parts[1])
-        diagonal = select_left(uses[0], own_one * a, 2) + select_left(uses[1], own_two * b, 2)
+        own = jnp.concatenate([own_one * a, own_two * b], axis=0)
+        diagonal = select_left(jnp.concatenate([uses[0], uses[1]], axis=1), own, 2)
         change = product(nets, flux)
         divisor = 1.0 - factor * diagonal
         fd = factor / divisor

time: 67.7 us -> 66.4 us (0.981)
  Pallas kernels: 37 us -> 56.7 us
  starting transfers between devices: 20.7 us -> 7.95 us
  waiting for transfers between devices: 9.79 us -> 1.11 us
    ppermute x4, starting transfers between devices: 20.7 us -> 7.95 us  [exchanged(): return lax.ppermute(value, 'tile', pairs + [(j, i) for i, j in pairs])]
    pallas_call x1, Pallas kernels: 16.1 us -> 27.4 us  [per_device(): pl.pallas_call(edge_kernel, out_shape=[shape(lists, LANES, dtype=jnp.int3...]
    ppermute x4, waiting for transfers between devices: 9.79 us -> 1.11 us  [exchanged(): return lax.ppermute(value, 'tile', pairs + [(j, i) for i, j in pairs])]
    pallas_call x1, Pallas kernels: 2.28 us -> 10.9 us  [per_device(): pl.pallas_call(functools.partial(later_kernel, real), out_shape=[state, m...]
  transfers between devices with their start and end apart: 4 -> 4, of which waited for: 1 -> 1; matrix products, arithmetic and copies ran while one was open for 0% -> 0% of each run, Pallas kernels for 21% -> 34%
where the time goes in v2:
time: 66.4 us; the launch traced here: 66.8 us
  Pallas kernels  56.7 us (85%)
  starting transfers between devices  7.95 us (12%)
  waiting for transfers between devices  1.11 us (2%)
  between operations  0.97 us (1%)
    pallas_call x1, Pallas kernels, per_device(): pl.pallas_call(edge_kernel, out_shape=[shape(lists, LANES, dtype=jnp.int3...  27.4 us
    pallas_call x1, Pallas kernels, per_device(): pl.pallas_call(functools.partial(inner_kernel, real), out_shape=[state, w...  11.9 us
    pallas_call x1, Pallas kernels, per_device(): pl.pallas_call(functools.partial(later_kernel, real), out_shape=[state, m...  10.9 us
    ppermute x4, starting transfers between devices, exchanged(): return lax.ppermute(value, 'tile', pairs + [(j, i) for i, j in pairs])  7.95 us
    pallas_call x1, Pallas kernels, per_device(): pl.pallas_call(advect_kernel, out_shape=[shape(group, species, halves, LA...  5.82 us
  transfers between devices with their start and end apart: 4, of which 1 were waited for; matrix products, arithmetic and copies ran while one was open for 0% of the time, Pallas kernels for 34%

profile of v2, /device:TPU:13, one launch (start us, length us, event | category | flops | bytes accessed | tf_op | source)
XLA Modules:
  0.0 66.8 jit_solution(17057471397084622758)
XLA Ops:
  0.6 0.0 copy-start
  0.6 0.0 copy-start.1
  0.7 0.0 copy-start.4
  0.7 0.0 copy-start.5
  0.7 0.0 copy-start.6
  0.7 27.4 %edge_columns.1 = (s32[8,128]{1,0:T(8,128)S(1)}, f32[8,128]{1,0:T(8,128)S(1)}, f32[8,256]{1,0:T(8,128)S(1)}, f32[130,256]{1,0:T(8,128)S(1)}, f32[4192,128]{1,0:T...) custom-call(s32[32]{0:T(128)} %chosen.3, ...), custom_call_target="tpu_custom_call" | custom-call | tf_op jit(solution)/shard_map/edge_columns/pallas_call | solution.py:686
  28.1 0.1 collective-permute-start
  28.2 3.2 %collective-permute-start.1 = (f32[1080,128]{1,0:T(8,128)S(1)}, f32[1080,128]{1,0:T(8,128)S(1)}, u32[]{:S(2)}, u32[]{:S(2)}) collective-permute-start(f32[1080,128]{1,0:T(8,128)S(1)} %get-tuple-element.26.s1), channel_id=1, source_target_pairs={{8,16},{10,18},{12,20},{14,22},{16,8},{18,10},{20,12},{22,14},{9,1... | collective-permute-start | bytes 1658888 | tf_op jit(solution)/shard_map/ppermute | solution.py:649
  31.4 0.0 copy-done
  31.4 0.0 copy-done.1
  31.4 0.0 copy-done.4
  31.4 0.0 copy-done.5
  31.4 0.0 copy-done.6
  31.4 11.9 %inner_columns.1 = (f32[4192,128]{1,0:T(8,128)S(1)}, f32[1080,256]{1,0:T(8,128)S(1)}, bf16[256,256]{1,0:T(8,128)(2,1)S(1)}, bf16[256,256]{1,0:T(8,128)(2,1)S(1)}) custom-call(s32[1024]{0:T(1024)S(1)} %bitcast.11, f32[1024]{0:T(1024)S(1)} %bitcast.13, s32[32]{0:T(128)S(1)} %copy-done.5, f32[8,256]{1,0:T(8,128)S(1)} %get-tuple-element.29.counts, ...), custom_call_target="tpu_custom_call" | custom-call | tf_op jit(solution)/shard_map/inner_columns/pallas_call | solution.py:739
  43.4 0.0 copy-start.2
  43.4 0.0 copy-start.3
  43.4 0.0 copy-start.7
  43.4 0.0 collective-permute-done.one.h0
  43.4 0.0 collective-permute-done.1.two.h1
  43.4 0.6 y_edges.1
  44.1 2.1 %collective-permute-start.2 = (f32[1080,128]{1,0:T(8,128)S(1)}, f32[1080,128]{1,0:T(8,128)S(1)}, u32[]{:S(2)}, u32[]{:S(2)}) collective-permute-start(f32[1080,128]{1,0:T(8,128)S(1)} %get-tuple-element.37), channel_id=1, source_target_pairs={{2,4},{6,8},{10,12},{14,16},{18,20},{22,24},{26,28},{4,2},{8,6},{1... | collective-permute-start | bytes 1658888 | tf_op jit(solution)/shard_map/ppermute | solution.py:649
  46.2 2.6 %collective-permute-start.3 = (f32[1080,128]{1,0:T(8,128)S(1)}, f32[1080,128]{1,0:T(8,128)S(1)}, u32[]{:S(2)}, u32[]{:S(2)}) collective-permute-start(f32[1080,128]{1,0:T(8,128)S(1)} %get-tuple-element.38), channel_id=1, source_target_pairs={{0,2},{4,6},{8,10},{12,14},{16,18},{20,22},{24,26},{28,30},{2,0},{... | collective-permute-start | bytes 1658888 | tf_op jit(solution)/shard_map/ppermute | solution.py:649
  48.7 0.0 copy-done.2
  48.7 0.0 copy-done.3
  48.7 0.0 copy-done.7
  48.7 10.9 %inner_later.1 = (f32[4192,128]{1,0:T(8,128)S(1)}, bf16[384,256]{1,0:T(8,128)(2,1)S(1)}, bf16[384,256]{1,0:T(8,128)(2,1)S(1)}) custom-call(s32[1024]{0:T(1024)S(1)} %bitcast.12, f32[1024]{0:T(1024)S(1)} %bitcast.14, s32[32]{0:T(128)S(1)} %copy-done.5, f32[8,256]{1,0:T(8,128)S(1)} %get-tuple-element.29.counts, f32[4,135,8,128]{3,2,1,0:T(8,128)S(1)} %get-tuple-element.32.held, ...), custom_call_target="tpu_custom_call" | custom-call | tf_op jit(solution)/shard_map/inner_later/pallas_call | solution.py:765
  59.7 1.1 %collective-permute-done.2.h3 = f32[1080,128]{1,0:T(8,128)S(1)} collective-permute-done((f32[1080,128]{1,0:T(8,128)S(1)}, f32[1080,128]{1,0:T(8,128)S(1)}, u32[]{:S(2)}, u32[]{:S(2)}) %collective-permute-start.2) | collective-permute-done | bytes 552992 | tf_op jit(solution)/shard_map/ppermute | solution.py:649
  60.8 0.0 collective-permute-done.3.h2
  60.8 5.8 %advection.1 = (f32[32,130,2,128]{3,2,1,0:T(2,128)}, f32[130,2,128]{2,1,0:T(2,128)}) custom-call(f32[130,256]{1,0:T(8,128)S(1)} %get-tuple-element.24.conc, f32[1080,128]{1,0:T(8,128)S(1)} %collective-permute-done.one.h0, f32[1080,128]{1,0:T(8,128)S(1)} %collective-permute-done.1.two.h1, f32[1080,128]{1,0:T(8,128)S(1)} %collective-permute-done.2.h3, ...), custom_call_target="tpu_custom_call" | custom-call | tf_op jit(solution)/shard_map/advection/pallas_call | solution.py:779
Async XLA Ops:
  0.6 30.8 %copy-start = (s32[768,3]{1,0:T(8,128)S(1)}, s32[768,3]{1,0:T(8,128)}, u32[]{:S(2)}) copy-start(s32[768,3]{1,0:T(8,128)} %constant.16.clone.side_in) | copy-start | bytes 27652
  0.6 30.8 %copy-start.1 = (f32[256,256]{1,0:T(8,128)S(1)}, f32[256,256]{1,0:T(8,128)}, u32[]{:S(2)}) copy-start(f32[256,256]{1,0:T(8,128)} %constant.15.clone.side_pick) | copy-start | bytes 786436
  0.7 30.8 %copy-start.4 = (f32[2,1,256]{2,1,0:T(1,128)S(1)}, f32[2,1,256]{2,1,0:T(1,128)}, u32[]{:S(2)}) copy-start(f32[2,1,256]{2,1,0:T(1,128)} %param.20) | copy-start | bytes 6148
  0.7 30.8 %copy-start.5 = (s32[32]{0:T(128)S(1)}, s32[32]{0:T(128)}, u32[]{:S(2)}) copy-start(s32[32]{0:T(128)} %chosen.3) | copy-start | bytes 388
  0.7 30.8 %copy-start.6 = (s32[3,256]{1,0:T(4,128)S(1)}, s32[3,256]{1,0:T(4,128)}, u32[]{:S(2)}) copy-start(s32[3,256]{1,0:T(4,128)} %constant.17.clone.side_out) | copy-start | bytes 9220
  28.1 15.3 %collective-permute-start = (f32[1080,128]{1,0:T(8,128)S(1)}, f32[1080,128]{1,0:T(8,128)S(1)}, u32[]{:S(2)}, u32[]{:S(2)}) collective-permute-start(f32[1080,128]{1,0:T(8,128)S(1)} %get-tuple-element.25.s0), channel_id=1, source_target_pairs={{0,8},{2,10},{4,12},{6,14},{16,24},{18,26},{20,28},{22,30},{8,0},{... | collective-permute-start | bytes 1658888 | tf_op jit(solution)/shard_map/ppermute | solution.py:649
  28.2 15.2 %collective-permute-start.1 = (f32[1080,128]{1,0:T(8,128)S(1)}, f32[1080,128]{1,0:T(8,128)S(1)}, u32[]{:S(2)}, u32[]{:S(2)}) collective-permute-start(f32[1080,128]{1,0:T(8,128)S(1)} %get-tuple-element.26.s1), channel_id=1, source_target_pairs={{8,16},{10,18},{12,20},{14,22},{16,8},{18,10},{20,12},{22,14},{9,1... | collective-permute-start | bytes 1658888 | tf_op jit(solution)/shard_map/ppermute | solution.py:649
  43.4 5.4 %copy-start.2 = (s32[384,2]{1,0:T(8,128)S(1)}, s32[384,2]{1,0:T(8,128)}, u32[]{:S(2)}) copy-start(s32[384,2]{1,0:T(8,128)} %constant.18.clone.entries) | copy-start | bytes 9220
  43.4 5.4 %copy-start.3 = (s32[256,2]{1,0:T(8,128)S(1)}, s32[256,2]{1,0:T(8,128)}, u32[]{:S(2)}) copy-start(s32[256,2]{1,0:T(8,128)} %constant.19.clone.cells) | copy-start | bytes 6148
  43.4 5.4 %copy-start.7 = (s32[2,256]{1,0:T(2,128)S(1)}, s32[2,256]{1,0:T(2,128)}, u32[]{:S(2)}) copy-start(s32[2,256]{1,0:T(2,128)} %constant.20.clone.cells_rows) | copy-start | bytes 6148
  44.1 16.7 %collective-permute-start.2 = (f32[1080,128]{1,0:T(8,128)S(1)}, f32[1080,128]{1,0:T(8,128)S(1)}, u32[]{:S(2)}, u32[]{:S(2)}) collective-permute-start(f32[1080,128]{1,0:T(8,128)S(1)} %get-tuple-element.37), channel_id=1, source_target_pairs={{2,4},{6,8},{10,12},{14,16},{18,20},{22,24},{26,28},{4,2},{8,6},{1... | collective-permute-start | bytes 1658888 | tf_op jit(solution)/shard_map/ppermute | solution.py:649
  46.2 14.6 %collective-permute-start.3 = (f32[1080,128]{1,0:T(8,128)S(1)}, f32[1080,128]{1,0:T(8,128)S(1)}, u32[]{:S(2)}, u32[]{:S(2)}) collective-permute-start(f32[1080,128]{1,0:T(8,128)S(1)} %get-tuple-element.38), channel_id=1, source_target_pairs={{0,2},{4,6},{8,10},{12,14},{16,18},{20,22},{24,26},{28,30},{2,0},{... | collective-permute-start | bytes 1658888 | tf_op jit(solution)/shard_map/ppermute | solution.py:649
